TPU v7x, 32 devices: a whole 2x2x4 slice. The times are simulated.
32 devices in a mesh: grp: 2 (over y), mon: 4 (over z), pair: 2 (over x), sub: 2 (over core).
Axes of the slice: x: 2, y: 2, z: 4, core: 2. Of those that a mesh axis runs over, the one named last changes fastest.
Arguments:
- dfactors: bfloat16 [8192, 1024], P('mon', 'sub'), may hold values from -0.5 to 0.5
- block_mask: int32 [64, 1024], P('mon', 'sub'), may hold values 0 or 1
- base_flow: float32 [8192], P('mon'), may hold values from -5 to 5
- branch_row: int32 [1024], replicated, may hold values from 0 to 8191, as said below
- pair_slots: int32 [3072, 2], P(('grp', 'pair')), parts along dimension 0, may hold values from 0 to 1023, as said below
- pair_counts: int32 [4], P(('grp', 'pair')), parts along dimension 0, may hold values from 1 to 768, 1024 in all
Outputs:
- post_flows: bfloat16 [8192, 3072], P(('mon', 'sub'), ('grp', 'pair')), parts along dimension 1
There are 2 independent parts, one for each index of `grp`. A program takes and returns all parts, laid end to end along the dimension named above; an argument that names none is the same for every part. Nothing has to cross between parts.
Inputs may be any that keep to these rules, and one draw needn't show every extreme that they name: `branch_row`: all entries distinct. `pair_slots`: the two candidates of a slot differ; empty slots hold valid pairs too. `pair_counts`: the counts sum to 1024; an owner's live slots are its first ones.
All inputs are finite; a program needn't handle non-finite values. No bound on the sum of `block_mask` or of `pair_counts` on one device may be relied on, other than what follows from the above.
Results may differ from a plain program's by a relative error of at most 0.004.
Values may be sent and summed in bfloat16 or wider, within the bound.
No kernel may reach another device: no remote copies, remote signals or barrier semaphores. Data moves between devices by JAX's collectives and lax.ppermute only.
A program may use at most 64 MiB of HBM per device.

v0:
```python
import functools

import jax
import jax.numpy as jnp
from jax import lax
from jax.experimental import pallas as pl
from jax.experimental.pallas import tpu as pltpu
from jax.sharding import PartitionSpec as P

BLOCK = 128
LANES = 128
SUBLANES = 8
ENDS = 256
VMEM_LIMIT = 16 * 1024 * 1024
F32 = jnp.float32
BF16 = jnp.bfloat16
I32 = jnp.int32


def chunk_of(total, want):
    size = min(total, want)
    while total % size:
        size -= BLOCK
    return size


def dense_rows(cap):
    return -(-cap // (LANES * SUBLANES)) * SUBLANES


def one_hot(hit):
    return jnp.where(hit, 1.0, 0.0).astype(BF16)


def iota(shape, axis):
    return lax.broadcasted_iota(I32, shape, axis)


def dense(line):
    cap = line.shape[1]
    rows = dense_rows(cap)
    pieces = [line[:, c : c + LANES] for c in range(0, cap, LANES)]
    if len(pieces) < rows:
        pieces.append(jnp.zeros((rows - len(pieces), LANES), line.dtype))
    return jnp.concatenate(pieces, axis=0)


def look_up(table, index):
    high, low = index >> 7, index & 127
    found = jnp.zeros(index.shape, table.dtype)
    for b in range(table.shape[0]):
        line = jnp.broadcast_to(table[b : b + 1], index.shape)
        value = jnp.take_along_axis(line, low, axis=1, mode="promise_in_bounds")
        found = jnp.where(high == b, value, found)
    return found


def values_kernel(
    n_sub, d_hbm, mask_hbm, base_hbm, rows_hbm, slots_hbm, *refs
):
    share_ref, *note_refs = refs[:n_sub]
    (
        d_ref, mask_ref, base_ref, slots_ref, rows_ref, perm_ref, hot_ref, cross_ref, sems, d_sems
    ) = refs[n_sub:]
    rows_dev, cols = d_ref.shape
    chunks = d_sems.shape[0]
    chunk = rows_dev // chunks
    cap = slots_ref.shape[1]
    lines = cap // LANES
    rows = dense_rows(cap)
    sub_index = lax.axis_index("sub")
    small = [
        pltpu.make_async_copy(src, dst, sems.at[i])
        for i, (src, dst) in enumerate(
            [(slots_hbm, slots_ref), (rows_hbm, rows_ref), (base_hbm, base_ref), (mask_hbm, mask_ref)]
        )
    ]
    large = [
        pltpu.make_async_copy(
            d_hbm.at[pl.ds(i * chunk, chunk)], d_ref.at[pl.ds(i * chunk, chunk)], d_sems.at[i]
        )
        for i in range(chunks)
    ]
    for copy in small + large:
        copy.start()

    small[0].wait()
    small[1].wait()
    first, second = dense(slots_ref[0:1, :]), dense(slots_ref[1:2, :])
    table = rows_ref[...]
    row = jnp.concatenate([look_up(table, first), look_up(table, second)], axis=0)
    row = row - lax.axis_index("mon") * rows_dev
    col = jnp.concatenate([second, first], axis=0) - sub_index * cols
    used = lax.rem(iota(row.shape, 0), rows) < lines
    here = used & (row >= 0) & (row < rows_dev) & (col >= 0) & (col < cols)

    flags = one_hot(here)
    height = flags.shape[0]
    above = jnp.dot(
        one_hot(iota((height, height), 1) < iota((height, height), 0)),
        flags,
        preferred_element_type=F32,
    ).astype(BF16)
    place = jnp.dot(
        jnp.concatenate([flags, above], axis=1),
        jnp.concatenate(
            [
                one_hot(iota((LANES, LANES), 0) <= iota((LANES, LANES), 1)),
                jnp.ones((LANES, LANES), BF16),
            ],
            axis=0,
        ),
        preferred_element_type=F32,
    ).astype(I32)
    place = jnp.where(here, place - 1, -1)
    digits = [(x >> shift) & 255 for x in (col, row) for shift in (0, 8)]
    order = [half * rows + b for half in range(2) for b in range(lines)]
    ends = jnp.concatenate(
        [jnp.concatenate([x[r : r + 1] for x in digits], axis=0) for r in order], axis=1
    )
    ends = ends.astype(F32).astype(BF16)

    def pick(start, copies=()):
        for at, r in enumerate(order):
            perm_ref[:, at * LANES : (at + 1) * LANES] = one_hot(
                iota((ENDS, LANES), 0) + start == place[r : r + 1]
            )
        packed = lax.dot_general(
            ends, perm_ref[...], (((1,), (1,)), ((), ())), preferred_element_type=F32
        ).astype(I32)
        end_col = packed[0:1] + (packed[1:2] << 8)
        end_row = packed[2:3] + (packed[3:4] << 8)
        hot_ref[...] = one_hot(iota((cols, ENDS), 0) == end_col)
        for copy in copies:
            copy.wait()
        keep = jnp.dot(
            mask_ref[...].astype(F32).astype(BF16), hot_ref[...], preferred_element_type=F32
        )
        keep = jnp.sum(
            jnp.where(iota(keep.shape, 0) == (end_row >> 7), keep, 0.0), axis=0, keepdims=True
        )
        total = jnp.zeros((SUBLANES, ENDS), F32)
        for i in range(chunks):
            values = jnp.dot(
                d_ref[i * chunk : (i + 1) * chunk, :], hot_ref[...], preferred_element_type=F32
            )
            picked = jnp.where(iota((chunk, ENDS), 0) + i * chunk == end_row, values, 0.0)
            total += jnp.sum(picked.reshape(chunk // SUBLANES, SUBLANES, ENDS), axis=0)
        value = jnp.sum(total, axis=0, keepdims=True) * keep
        value = jnp.concatenate([value[:, q : q + LANES] for q in range(0, ENDS, LANES)], axis=0)
        return look_up(value, place - start)

    def put(cross, flow):
        for ref in (share_ref, *note_refs):
            ref[: 2 * rows, :] = cross
            ref[2 * rows : 4 * rows, :] = flow

    cross = pick(0, small[2:] + large)
    flow = jnp.where(sub_index == 0, look_up(base_ref[...], row), 0.0)
    put(cross, flow)
    my_blocks = mask_ref.shape[0] // n_sub
    for s, ref in enumerate(note_refs, 1):
        block = pl.multiple_of(lax.rem(sub_index + s, n_sub) * my_blocks, my_blocks)
        for c in range(cols // LANES):
            at = 4 * rows + c * my_blocks
            ref[at : at + my_blocks, :] = mask_ref[
                pl.ds(block, my_blocks), c * LANES : (c + 1) * LANES
            ].astype(F32)
    count = jnp.max(place) + 1

    @pl.when(count > ENDS)
    def _():
        cross_ref[...] = cross

        def more(i, _):
            cross_ref[...] += pick(i * ENDS)
            return 0

        lax.fori_loop(1, pl.cdiv(count, ENDS), more, 0)
        put(cross_ref[...], flow)


def pick_columns(parts, slot, starts, cols, masked_ref, hot_ref, out_ref):
    width = hot_ref.shape[2]
    for part in parts:
        lanes = slice(part * width, (part + 1) * width)
        for s, start in enumerate(starts):
            hot_ref[part, s * cols : (s + 1) * cols, :] = one_hot(
                iota((cols, width), 0) == slot[:, lanes] - start
            )
        out_ref[:, lanes] = jnp.dot(
            masked_ref[...], hot_ref[part], preferred_element_type=F32
        ).astype(BF16)


def fewest(parts):
    return min(2, parts)


def live_parts(count, width, parts):
    return jnp.clip((count + width - 1) // width, fewest(parts), parts)


def is_early():
    return lax.axis_index("mon") < lax.axis_size("mon") // 2


def column_starts(n_sub, cols):
    return [lax.rem(lax.axis_index("sub") + n_sub - s, n_sub) * cols for s in range(n_sub)]


def mask_factors(n_sub, refs, masked_ref):
    d_refs, note_refs, mask_ref = refs[:n_sub], refs[n_sub:-1], refs[-1]
    my_rows, all_cols = masked_ref.shape
    cols = all_cols // n_sub
    my_blocks = my_rows // BLOCK
    sub_index = lax.axis_index("sub")
    my_start = pl.multiple_of(sub_index * my_rows, my_rows)
    my_block = pl.multiple_of(sub_index * my_blocks, my_blocks)
    for s in range(n_sub):
        if s == 0:
            keep = mask_ref[pl.ds(my_block, my_blocks), :].astype(F32)
        else:
            ref = note_refs[s - 1]
            ends = range(ref.shape[0] - (cols // LANES) * my_blocks, ref.shape[0], my_blocks)
            keep = jnp.concatenate([ref[at : at + my_blocks, :] for at in ends], axis=1)
        keep = keep.astype(BF16)
        for b in range(my_blocks):
            masked_ref[b * BLOCK : (b + 1) * BLOCK, s * cols : (s + 1) * cols] = (
                d_refs[s][pl.ds(my_start + b * BLOCK, BLOCK), :] * keep[b : b + 1]
            )


def early_kernel(n_sub, *refs):
    *factor_refs, slots_ref, share_ref, masked_ref, first_ref, shared_ref, hot_ref = refs
    shared_ref[...] = share_ref[...]
    cols = masked_ref.shape[1] // n_sub

    @pl.when(is_early())
    def _():
        mask_factors(n_sub, factor_refs, masked_ref)
        starts = column_starts(n_sub, cols)
        pick_columns([0], slots_ref[0:1, :], starts, cols, masked_ref, hot_ref, first_ref)


def first_kernel(n_sub, *refs):
    *factor_refs, slots_ref, count_ref, _, _, masked_ref, first_ref, hot_ref = refs
    cols = masked_ref.shape[1] // n_sub
    slot = slots_ref[0:1, :]
    starts = column_starts(n_sub, cols)
    parts, _, width = hot_ref.shape
    live = live_parts(count_ref[0], width, parts)
    for n_parts in range(fewest(parts), parts + 1):

        @pl.when((live == n_parts) & jnp.logical_not(is_early()))
        def _():
            mask_factors(n_sub, factor_refs, masked_ref)
            pick_columns(range(n_parts), slot, starts, cols, masked_ref, hot_ref, first_ref)

        @pl.when((live == n_parts) & is_early())
        def _():
            pick_columns(range(1, n_parts), slot, starts, cols, masked_ref, hot_ref, first_ref)


def second_kernel(
    n_sub, masked_ref, slots_ref, count_ref, second_ref, out_hbm, hot_ref, zero_ref, sems
):
    cols = masked_ref.shape[1] // n_sub
    slot = slots_ref[1:2, :]
    starts = column_starts(n_sub, cols)
    parts, _, width = hot_ref.shape
    live = live_parts(count_ref[0], width, parts)
    for n_parts in range(fewest(parts), parts + 1):

        @pl.when(live == n_parts)
        def _():
            copies = [
                pltpu.make_async_copy(
                    zero_ref, out_hbm.at[:, part * width : (part + 1) * width], sems.at[part]
                )
                for part in range(n_parts, parts)
            ]
            if copies:
                zero_ref[...] = jnp.zeros_like(zero_ref)
            for copy in copies:
                copy.start()
            pick_columns(range(n_parts), slot, starts, cols, masked_ref, hot_ref, second_ref)
            for copy in copies:
                copy.wait()


def flows_kernel(n_shares, width, *refs):
    share_refs, refs = refs[:n_shares], refs[n_shares:]
    base_ref, first_ref, second_ref, count_ref, _, out_hbm, post_ref, out_sems = refs
    my_rows, cap = post_ref.shape
    my_blocks = my_rows // BLOCK
    rows = dense_rows(cap)
    total = share_refs[0][...]
    for ref in share_refs[1:]:
        total = total + ref[...]
    cross_first, cross_second, flow_first, flow_second = (
        total[i * rows : (i + 1) * rows] for i in range(4)
    )
    determinant = 1.0 - cross_first * cross_second
    shift_first = (flow_first + cross_first * flow_second) / determinant
    shift_second = (flow_second + cross_second * flow_first) / determinant
    my_block = pl.multiple_of(lax.axis_index("sub") * my_blocks, my_blocks)
    base = jnp.swapaxes(base_ref[pl.ds(my_block, my_blocks), :], 0, 1)

    def write(lines):
        live = [iota((1, LANES), 1) + line * LANES < count_ref[0] for line in lines]
        weights = [
            [
                jnp.broadcast_to(shift[line : line + 1], (BLOCK, LANES)).astype(BF16)
                for line in lines
            ]
            for shift in (shift_first, shift_second)
        ]
        wide = slice(0, len(lines) * LANES)
        out_copies = []
        for b in range(my_blocks):
            block = slice(b * BLOCK, (b + 1) * BLOCK)
            start = jnp.broadcast_to(base[:, b : b + 1], (BLOCK, LANES))
            for line in lines:
                lanes = slice(line * LANES, (line + 1) * LANES)
                change = (
                    weights[0][line] * first_ref[block, lanes]
                    + weights[1][line] * second_ref[block, lanes]
                )
                post_ref[block, lanes] = jnp.where(
                    live[line], start + change.astype(F32), 0.0
                ).astype(BF16)
            out_copies.append(
                pltpu.make_async_copy(
                    post_ref.at[block, wide], out_hbm.at[block, wide], out_sems.at[b]
                )
            )
            out_copies[-1].start()
        for copy in out_copies:
            copy.wait()

    parts = cap // width
    live_count = live_parts(count_ref[0], width, parts)
    for n_parts in range(fewest(parts), parts + 1):
        pl.when(live_count == n_parts)(
            functools.partial(write, range(n_parts * width // LANES))
        )


def partners(n_mon):
    half = n_mon // 2
    if n_mon & (n_mon - 1):
        return [[(m + k) % n_mon for m in range(n_mon)] for k in range(1, n_mon)]
    across = [
        [m ^ (half + k) if m < half else m ^ (n_mon - 1 - k) for m in range(n_mon)]
        for k in range(half)
    ]
    return across + [[m ^ k for m in range(n_mon)] for k in range(half - 1, 0, -1)]


def from_other_mon(share, n_mon, n_sub):
    return [
        lax.ppermute(
            share,
            ("mon", "sub"),
            [
                (m * n_sub + s, to[m] * n_sub + n_sub - 1 - s)
                for m in range(n_mon)
                for s in range(n_sub)
            ],
        )
        for to in reversed(partners(n_mon))
    ]


def on_device(dfactors, block_mask, base_flow, branch_row, pair_slots, pair_counts):
    rows_dev, cols = dfactors.shape
    blocks = rows_dev // BLOCK
    candidates = branch_row.shape[0]
    cap = pair_slots.shape[0]
    rows = dense_rows(cap)
    n_sub = lax.axis_size("sub")
    my_rows = rows_dev // n_sub
    slots = pair_slots.T
    base = base_flow.reshape(blocks, BLOCK)
    table = branch_row.reshape(candidates // LANES, LANES)
    hbm = pl.BlockSpec(memory_space=pltpu.HBM)
    in_hbm = functools.partial(pltpu.with_memory_space_constraint, memory_space=pltpu.HBM)
    in_vmem = functools.partial(pltpu.with_memory_space_constraint, memory_space=pltpu.VMEM)
    vmem = pl.BlockSpec(memory_space=pltpu.VMEM)
    smem = pl.BlockSpec(memory_space=pltpu.SMEM)
    params = pltpu.CompilerParams(vmem_limit_bytes=VMEM_LIMIT)
    rings = [[(i, (i + s) % n_sub) for i in range(n_sub)] for s in range(n_sub)]

    factors = [dfactors] + [lax.ppermute(dfactors, "sub", ring) for ring in rings[1:]]

    chunks = rows_dev // chunk_of(rows_dev, 512)
    note_rows = 4 * rows + (cols // LANES) * (my_rows // BLOCK)
    outs = pl.pallas_call(
        functools.partial(values_kernel, n_sub),
        out_shape=[pltpu.VMEM((4 * rows, LANES), F32)]
        + [pltpu.VMEM((note_rows, LANES), F32)] * (n_sub - 1)
        + [
            pltpu.VMEM((rows_dev, cols), BF16),
            pltpu.VMEM((blocks, cols), I32),
            pltpu.VMEM((blocks, BLOCK), F32),
            pltpu.VMEM((2, cap), I32),
        ],
        in_specs=[hbm] * 5,
        out_specs=[vmem] * (n_sub + 4),
        scratch_shapes=[
            pltpu.VMEM((candidates // LANES, LANES), I32),
            pltpu.VMEM((ENDS, 2 * cap), BF16),
            pltpu.VMEM((cols, ENDS), BF16),
            pltpu.VMEM((2 * rows, LANES), F32),
            pltpu.SemaphoreType.DMA((4,)),
            pltpu.SemaphoreType.DMA((chunks,)),
        ],
        compiler_params=params,
        cost_estimate=pl.CostEstimate(
            flops=2 * rows_dev * cols * ENDS, bytes_accessed=rows_dev * cols * 2, transcendentals=0
        ),
        name="pair_values",
    )(*map(in_hbm, (dfactors, block_mask, base, table, slots)))
    share, notes = outs[0], outs[1:n_sub]
    factors[0], block_mask, base, slots = outs[n_sub:]

    notes = [lax.ppermute(note, "sub", ring) for note, ring in zip(notes, rings[1:])]
    share = functools.reduce(jnp.add, [share] + [note[: 4 * rows] for note in notes])
    width = chunk_of(cap, 256)
    hot = pltpu.VMEM((cap // width, n_sub * cols, width), BF16)
    columns = pltpu.VMEM((my_rows, cap), BF16)
    masked = pltpu.VMEM((my_rows, n_sub * cols), BF16)
    columns_cost = pl.CostEstimate(
        flops=2 * my_rows * cols * n_sub * cap,
        bytes_accessed=my_rows * (cols * n_sub + cap) * 2,
        transcendentals=0,
    )
    factors = [*factors, *notes, block_mask]
    masked, first, share = pl.pallas_call(
        functools.partial(early_kernel, n_sub),
        out_shape=[masked, columns, pltpu.VMEM(share.shape, F32)],
        in_specs=[vmem] * (len(factors) + 2),
        out_specs=[vmem] * 3,
        scratch_shapes=[hot],
        compiler_params=params,
        name="early_columns",
    )(*map(in_vmem, (*factors, slots, share)))
    shares = [share, *from_other_mon(share, lax.axis_size("mon"), n_sub)]

    masked, first = pl.pallas_call(
        functools.partial(first_kernel, n_sub),
        out_shape=[pltpu.VMEM(masked.shape, BF16), columns],
        in_specs=[vmem] * (len(factors) + 1) + [smem] + [vmem] * 2,
        out_specs=[vmem] * 2,
        input_output_aliases={len(factors) + 2: 0, len(factors) + 3: 1},
        scratch_shapes=[hot],
        compiler_params=params,
        cost_estimate=columns_cost,
        name="first_columns",
    )(*map(in_vmem, (*factors, slots)), pair_counts, *map(in_vmem, (masked, first)))
    second, out = pl.pallas_call(
        functools.partial(second_kernel, n_sub),
        out_shape=[columns, pltpu.HBM((my_rows, cap), BF16)],
        in_specs=[vmem] * 2 + [smem],
        out_specs=[vmem, hbm],
        scratch_shapes=[
            hot,
            pltpu.VMEM((my_rows, width), BF16),
            pltpu.SemaphoreType.DMA((cap // width,)),
        ],
        compiler_params=params,
        cost_estimate=columns_cost,
        name="second_columns",
    )(*map(in_vmem, (masked, slots)), pair_counts)
    return pl.pallas_call(
        functools.partial(flows_kernel, len(shares), width),
        out_shape=jax.ShapeDtypeStruct((my_rows, cap), BF16),
        in_specs=[vmem] * (len(shares) + 3) + [smem, hbm],
        out_specs=hbm,
        input_output_aliases={len(shares) + 4: 0},
        scratch_shapes=[
            pltpu.VMEM((my_rows, cap), BF16),
            pltpu.SemaphoreType.DMA((my_rows // BLOCK,)),
        ],
        compiler_params=params,
        cost_estimate=pl.CostEstimate(
            flops=6 * my_rows * cap, bytes_accessed=my_rows * cap * 2, transcendentals=0
        ),
        name="post_flows",
    )(*map(in_vmem, (*shares, base, first, second)), pair_counts, in_hbm(out))


def solution(mesh):
    return jax.shard_map(
        on_device,
        mesh=mesh,
        in_specs=(
            P("mon", "sub"),
            P("mon", "sub"),
            P("mon"),
            P(),
            P(("grp", "pair"), None),
            P(("grp", "pair")),
        ),
        out_specs=P(("mon", "sub"), ("grp", "pair")),
        check_vma=False,
    )
```

profile of v0, /device:TPU:0, one launch (start us, length us, event | category | flops | bytes accessed | tf_op | source)
XLA Modules:
  0.0 14.6 jit_solution(15372277169892025134)
XLA Ops:
  0.0 0.5 %collective-permute-start = (bf16[2048,512]{1,0:T(8,128)(2,1)}, bf16[2048,512]{1,0:T(8,128)(2,1)S(1)}, u32[]{:S(2)}, u32[]{:S(2)}) collective-permute-start(bf16[2048,512]{1,0:T(8,128)(2,1)} %d_hbm.1), channel_id=1, source_target_pairs={{0,1},{1,0},{2,3},{3,2},{4,5},{5,4},{6,7},{7,6},{8,9},{9,8},{10,11... | collective-permute-start | bytes 6291464 | tf_op jit(solution)/shard_map/ppermute | solution.py:395
  0.5 3.0 %pair_values.1 = (f32[32,128]{1,0:T(8,128)S(1)}, f32[64,128]{1,0:T(8,128)S(1)}, bf16[2048,512]{1,0:T(8,128)(2,1)S(1)}, s32[16,512]{1,0:T(8,128)S(1)}, f32[16,128]{1,0:T(8,128)S(1)}, /*index=5*/s32[2,768]{1,0:T(2,128)S(1)}) custom-call(bf16[2048,512]{1,0:T(8,128)(2,1)} %d_hbm.1, s32[16,512]{1,0:T(8,128)} %mask_hbm.1, f32[16,128]{1,0:T(8,128)} %bitcast.3, ...), custom_call_target="tpu_custom_call" | custom-call | flops 536870912 | bytes 2097152 | tf_op jit(solution)/shard_map/pair_values/pallas_call | solution.py:399
  3.4 0.1 collective-permute-start.1
  4.2 0.5 %collective-permute-done.1.refs_2_ = f32[64,128]{1,0:T(8,128)S(1)} collective-permute-done((f32[64,128]{1,0:T(8,128)S(1)}, f32[64,128]{1,0:T(8,128)S(1)}, u32[]{:S(2)}, u32[]{:S(2)}) %collective-permute-start.1) | collective-permute-done | bytes 32800 | tf_op jit(solution)/shard_map/ppermute | solution.py:428
  4.7 0.0 collective-permute-done.refs_1_
  4.7 0.8 %early_columns.1 = (bf16[1024,1024]{1,0:T(8,128)(2,1)S(1)}, bf16[1024,768]{1,0:T(8,128)(2,1)S(1)}, f32[32,128]{1,0:T(8,128)S(1)}) custom-call(bf16[2048,512]{1,0:T(8,128)(2,1)S(1)} %get-tuple-element.18.refs_0_, bf16[2048,512]{1,0:T(8,128)(2,1)S(1)} %collective-permute-done.refs_1_, f32[64,128]{1,0:T(8,128)S(1)} %collective-permute-done.1.refs_2_, ...), custom_call_target="tpu_custom_call" | custom-call | tf_op jit(solution)/shard_map/early_columns/pallas_call | solution.py:440
  5.5 3.0 %collective-permute-start.4 = (f32[32,128]{1,0:T(8,128)S(1)}, f32[32,128]{1,0:T(8,128)S(1)}, u32[]{:S(2)}, u32[]{:S(2)}) collective-permute-start(f32[32,128]{1,0:T(8,128)S(1)} %get-tuple-element.23.refs_0_), channel_id=1, source_target_pairs={{0,9},{1,8},{4,13},{5,12},{8,5},{9,4},{12,1},{13,0},{2,11},{3,10},... | collective-permute-start | bytes 49160 | tf_op jit(solution)/shard_map/ppermute | solution.py:363
  8.5 1.1 %collective-permute-start.3 = (f32[32,128]{1,0:T(8,128)S(1)}, f32[32,128]{1,0:T(8,128)S(1)}, u32[]{:S(2)}, u32[]{:S(2)}) collective-permute-start(f32[32,128]{1,0:T(8,128)S(1)} %get-tuple-element.23.refs_0_), channel_id=1, source_target_pairs={{0,13},{1,12},{4,9},{5,8},{8,1},{9,0},{12,5},{13,4},{2,15},{3,14},... | collective-permute-start | bytes 49160 | tf_op jit(solution)/shard_map/ppermute | solution.py:363
  9.6 0.4 %collective-permute-start.2 = (f32[32,128]{1,0:T(8,128)S(1)}, f32[32,128]{1,0:T(8,128)S(1)}, u32[]{:S(2)}, u32[]{:S(2)}) collective-permute-start(f32[32,128]{1,0:T(8,128)S(1)} %get-tuple-element.23.refs_0_), channel_id=1, source_target_pairs={{0,5},{1,4},{4,1},{5,0},{8,13},{9,12},{12,9},{13,8},{2,7},{3,6},{6... | collective-permute-start | bytes 49160 | tf_op jit(solution)/shard_map/ppermute | solution.py:363
  9.9 1.3 %first_columns.1 = (bf16[1024,1024]{1,0:T(8,128)(2,1)S(1)}, bf16[1024,768]{1,0:T(8,128)(2,1)S(1)}) custom-call(bf16[2048,512]{1,0:T(8,128)(2,1)S(1)} %get-tuple-element.18.refs_0_, bf16[2048,512]{1,0:T(8,128)(2,1)S(1)} %collective-permute-done.refs_1_, f32[64,128]{1,0:T(8,128)S(1)} %collective-permute-done.1.refs_2_, ...), custom_call_target="tpu_custom_call", output_to_operand_aliasing={{0}: (6, {}), {1}: (7, {})} | custom-call | flops 1610612736 | bytes 3670016 | tf_op jit(solution)/shard_map/first_columns/pallas_call | solution.py:451
  11.2 1.8 %second_columns.1 = (bf16[1024,768]{1,0:T(8,128)(2,1)S(1)}, bf16[1024,768]{1,0:T(8,128)(2,1)}) custom-call(bf16[1024,1024]{1,0:T(8,128)(2,1)S(1)} %get-tuple-element.28.masked_ref, s32[2,768]{1,0:T(2,128)S(1)} %get-tuple-element.21.refs_4_.slots_ref, s32[1]{0:T(128)S(6)} %copy.13.refs_5_.count_ref.refs_7_), custom_call_target="tpu_custom_call" | custom-call | flops 1610612736 | bytes 3670016 | tf_op jit(solution)/shard_map/second_columns/pallas_call | solution.py:462
  13.1 0.0 collective-permute-done.4.refs_3_
  13.1 0.0 collective-permute-done.3.refs_2_
  13.1 0.0 collective-permute-done.2.refs_1_
  13.1 1.5 %post_flows.1 = bf16[1024,768]{1,0:T(8,128)(2,1)} custom-call(f32[32,128]{1,0:T(8,128)S(1)} %get-tuple-element.23.refs_0_, f32[32,128]{1,0:T(8,128)S(1)} %collective-permute-done.2.refs_1_, f32[32,128]{1,0:T(8,128)S(1)} %collective-permute-done.3.refs_2_, f32[32,128]{1,0:T(8,128)S(1)} %collective-permute-done.4.refs_3_, ...), custom_call_target="tpu_custom_call", output_to_operand_aliasing={{}: (8, {})} | custom-call | flops 4718592 | bytes 1572864 | tf_op jit(solution)/shard_map/post_flows/pallas_call | solution.py:476
  (1 shorter events, 0.0 us)
Async XLA Ops:
  0.0 4.7 %collective-permute-start = (bf16[2048,512]{1,0:T(8,128)(2,1)}, bf16[2048,512]{1,0:T(8,128)(2,1)S(1)}, u32[]{:S(2)}, u32[]{:S(2)}) collective-permute-start(bf16[2048,512]{1,0:T(8,128)(2,1)} %d_hbm.1), channel_id=1, source_target_pairs={{0,1},{1,0},{2,3},{3,2},{4,5},{5,4},{6,7},{7,6},{8,9},{9,8},{10,11... | collective-permute-start | bytes 6291464 | tf_op jit(solution)/shard_map/ppermute | solution.py:395
  3.4 1.3 %collective-permute-start.1 = (f32[64,128]{1,0:T(8,128)S(1)}, f32[64,128]{1,0:T(8,128)S(1)}, u32[]{:S(2)}, u32[]{:S(2)}) collective-permute-start(f32[64,128]{1,0:T(8,128)S(1)} %get-tuple-element.19), channel_id=1, source_target_pairs={{0,1},{1,0},{2,3},{3,2},{4,5},{5,4},{6,7},{7,6},{8,9},{9,8},{10,11... | collective-permute-start | bytes 98312 | tf_op jit(solution)/shard_map/ppermute | solution.py:428
  5.5 7.6 %collective-permute-start.4 = (f32[32,128]{1,0:T(8,128)S(1)}, f32[32,128]{1,0:T(8,128)S(1)}, u32[]{:S(2)}, u32[]{:S(2)}) collective-permute-start(f32[32,128]{1,0:T(8,128)S(1)} %get-tuple-element.23.refs_0_), channel_id=1, source_target_pairs={{0,9},{1,8},{4,13},{5,12},{8,5},{9,4},{12,1},{13,0},{2,11},{3,10},... | collective-permute-start | bytes 49160 | tf_op jit(solution)/shard_map/ppermute | solution.py:363
  8.5 4.6 %collective-permute-start.3 = (f32[32,128]{1,0:T(8,128)S(1)}, f32[32,128]{1,0:T(8,128)S(1)}, u32[]{:S(2)}, u32[]{:S(2)}) collective-permute-start(f32[32,128]{1,0:T(8,128)S(1)} %get-tuple-element.23.refs_0_), channel_id=1, source_target_pairs={{0,13},{1,12},{4,9},{5,8},{8,1},{9,0},{12,5},{13,4},{2,15},{3,14},... | collective-permute-start | bytes 49160 | tf_op jit(solution)/shard_map/ppermute | solution.py:363
  9.6 3.5 %collective-permute-start.2 = (f32[32,128]{1,0:T(8,128)S(1)}, f32[32,128]{1,0:T(8,128)S(1)}, u32[]{:S(2)}, u32[]{:S(2)}) collective-permute-start(f32[32,128]{1,0:T(8,128)S(1)} %get-tuple-element.23.refs_0_), channel_id=1, source_target_pairs={{0,5},{1,4},{4,1},{5,0},{8,13},{9,12},{12,9},{13,8},{2,7},{3,6},{6... | collective-permute-start | bytes 49160 | tf_op jit(solution)/shard_map/ppermute | solution.py:363
where the time goes:
time: 14.6 us
  Pallas kernels  8.31 us (57%)
  starting transfers between devices  5.06 us (35%)
  between operations  0.71 us (5%)
  waiting for transfers between devices  0.51 us (3%)
    ppermute x3, starting transfers between devices, from_other_mon(): lax.ppermute(share, ('mon', 'sub'), [(m * n_sub + s, to[m] * n_sub + n_su...  4.48 us
    pallas_call x1, Pallas kernels, on_device(): pl.pallas_call(functools.partial(values_kernel, n_sub), out_shape=[pltpu....  2.96 us
    pallas_call x1, Pallas kernels, on_device(): pl.pallas_call(functools.partial(second_kernel, n_sub), out_shape=[column...  1.85 us
    pallas_call x1, Pallas kernels, on_device(): pl.pallas_call(functools.partial(flows_kernel, len(shares), width), out_s...  1.5 us
    pallas_call x1, Pallas kernels, on_device(): pl.pallas_call(functools.partial(first_kernel, n_sub), out_shape=[pltpu.V...  1.25 us
    pallas_call x1, Pallas kernels, on_device(): pl.pallas_call(functools.partial(early_kernel, n_sub), out_shape=[masked,...  0.75 us
    ppermute x1, waiting for transfers between devices, on_device(): lax.ppermute(note, 'sub', ring)  0.5 us
    ppermute x1, starting transfers between devices, on_device(): lax.ppermute(dfactors, 'sub', ring)  0.45 us
  transfers between devices with their start and end apart: 5, of which 1 were waited for; matrix products, arithmetic and copies ran while one was open for 0% of the time, Pallas kernels for 42%

commit v1 on v0

--- a/solution.py
+++ b/solution.py
@@ -131,7 +131,7 @@
         end_col = packed[0:1] + (packed[1:2] << 8)
         end_row = packed[2:3] + (packed[3:4] << 8)
         hot_ref[...] = one_hot(iota((cols, ENDS), 0) == end_col)
-        for copy in copies:
+        for copy in copies[:2]:
             copy.wait()
         keep = jnp.dot(
             mask_ref[...].astype(F32).astype(BF16), hot_ref[...], preferred_element_type=F32
@@ -139,6 +139,8 @@
         keep = jnp.sum(
             jnp.where(iota(keep.shape, 0) == (end_row >> 7), keep, 0.0), axis=0, keepdims=True
         )
+        for copy in copies[2:]:
+            copy.wait()
         total = jnp.zeros((SUBLANES, ENDS), F32)
         for i in range(chunks):
             values = jnp.dot(
@@ -307,20 +309,24 @@
     my_block = pl.multiple_of(lax.axis_index("sub") * my_blocks, my_blocks)
     base = jnp.swapaxes(base_ref[pl.ds(my_block, my_blocks), :], 0, 1)
 
+    per = 2
+    step = BLOCK // per
+
     def write(lines):
         live = [iota((1, LANES), 1) + line * LANES < count_ref[0] for line in lines]
         weights = [
             [
-                jnp.broadcast_to(shift[line : line + 1], (BLOCK, LANES)).astype(BF16)
+                jnp.broadcast_to(shift[line : line + 1], (step, LANES)).astype(BF16)
                 for line in lines
             ]
             for shift in (shift_first, shift_second)
         ]
         wide = slice(0, len(lines) * LANES)
         out_copies = []
-        for b in range(my_blocks):
-            block = slice(b * BLOCK, (b + 1) * BLOCK)
-            start = jnp.broadcast_to(base[:, b : b + 1], (BLOCK, LANES))
+        for b in range(my_rows // step):
+            block = slice(b * step, (b + 1) * step)
+            part, at = b // per, b % per * step
+            start = jnp.broadcast_to(base[at : at + step, part : part + 1], (step, LANES))
             for line in lines:
                 lanes = slice(line * LANES, (line + 1) * LANES)
                 change = (
@@ -481,7 +487,7 @@
         input_output_aliases={len(shares) + 4: 0},
         scratch_shapes=[
             pltpu.VMEM((my_rows, cap), BF16),
-            pltpu.SemaphoreType.DMA((my_rows // BLOCK,)),
+            pltpu.SemaphoreType.DMA((2 * my_rows // BLOCK,)),
         ],
         compiler_params=params,
         cost_estimate=pl.CostEstimate(

time: 14.6 us -> 14.8 us (1.014)
  Pallas kernels: 8.31 us -> 8.48 us
where the time goes in v1:
time: 14.8 us
  Pallas kernels  8.48 us (57%)
  starting transfers between devices  5.06 us (34%)
  between operations  0.71 us (5%)
  waiting for transfers between devices  0.51 us (3%)
    ppermute x3, starting transfers between devices, from_other_mon(): lax.ppermute(share, ('mon', 'sub'), [(m * n_sub + s, to[m] * n_sub + n_su...  4.48 us
    pallas_call x1, Pallas kernels, on_device(): pl.pallas_call(functools.partial(values_kernel, n_sub), out_shape=[pltpu....  3.09 us
    pallas_call x1, Pallas kernels, on_device(): pl.pallas_call(functools.partial(second_kernel, n_sub), out_shape=[column...  1.85 us
    pallas_call x1, Pallas kernels, on_device(): pl.pallas_call(functools.partial(flows_kernel, len(shares), width), out_s...  1.54 us
    pallas_call x1, Pallas kernels, on_device(): pl.pallas_call(functools.partial(first_kernel, n_sub), out_shape=[pltpu.V...  1.26 us
    pallas_call x1, Pallas kernels, on_device(): pl.pallas_call(functools.partial(early_kernel, n_sub), out_shape=[masked,...  0.75 us
    ppermute x1, waiting for transfers between devices, on_device(): lax.ppermute(note, 'sub', ring)  0.5 us
    ppermute x1, starting transfers between devices, on_device(): lax.ppermute(dfactors, 'sub', ring)  0.45 us
  transfers between devices with their start and end apart: 5, of which 1 were waited for; matrix products, arithmetic and copies ran while one was open for 0% of the time, Pallas kernels for 42%

profile of v1, /device:TPU:0, one launch (start us, length us, event | category | flops | bytes accessed | tf_op | source)
XLA Modules:
  0.0 14.8 jit_solution(3395890282299878010)
XLA Ops:
  0.0 0.5 %collective-permute-start = (bf16[2048,512]{1,0:T(8,128)(2,1)}, bf16[2048,512]{1,0:T(8,128)(2,1)S(1)}, u32[]{:S(2)}, u32[]{:S(2)}) collective-permute-start(bf16[2048,512]{1,0:T(8,128)(2,1)} %d_hbm.1), channel_id=1, source_target_pairs={{0,1},{1,0},{2,3},{3,2},{4,5},{5,4},{6,7},{7,6},{8,9},{9,8},{10,11... | collective-permute-start | bytes 6291464 | tf_op jit(solution)/shard_map/ppermute | solution.py:401
  0.5 3.1 %pair_values.1 = (f32[32,128]{1,0:T(8,128)S(1)}, f32[64,128]{1,0:T(8,128)S(1)}, bf16[2048,512]{1,0:T(8,128)(2,1)S(1)}, s32[16,512]{1,0:T(8,128)S(1)}, f32[16,128]{1,0:T(8,128)S(1)}, /*index=5*/s32[2,768]{1,0:T(2,128)S(1)}) custom-call(bf16[2048,512]{1,0:T(8,128)(2,1)} %d_hbm.1, s32[16,512]{1,0:T(8,128)} %mask_hbm.1, f32[16,128]{1,0:T(8,128)} %bitcast.3, ...), custom_call_target="tpu_custom_call" | custom-call | flops 536870912 | bytes 2097152 | tf_op jit(solution)/shard_map/pair_values/pallas_call | solution.py:405
  3.5 0.1 collective-permute-start.1
  4.3 0.5 %collective-permute-done.1.refs_2_ = f32[64,128]{1,0:T(8,128)S(1)} collective-permute-done((f32[64,128]{1,0:T(8,128)S(1)}, f32[64,128]{1,0:T(8,128)S(1)}, u32[]{:S(2)}, u32[]{:S(2)}) %collective-permute-start.1) | collective-permute-done | bytes 32800 | tf_op jit(solution)/shard_map/ppermute | solution.py:434
  4.8 0.0 collective-permute-done.refs_1_
  4.8 0.8 %early_columns.1 = (bf16[1024,1024]{1,0:T(8,128)(2,1)S(1)}, bf16[1024,768]{1,0:T(8,128)(2,1)S(1)}, f32[32,128]{1,0:T(8,128)S(1)}) custom-call(bf16[2048,512]{1,0:T(8,128)(2,1)S(1)} %get-tuple-element.18.refs_0_, bf16[2048,512]{1,0:T(8,128)(2,1)S(1)} %collective-permute-done.refs_1_, f32[64,128]{1,0:T(8,128)S(1)} %collective-permute-done.1.refs_2_, ...), custom_call_target="tpu_custom_call" | custom-call | tf_op jit(solution)/shard_map/early_columns/pallas_call | solution.py:446
  5.6 3.0 %collective-permute-start.4 = (f32[32,128]{1,0:T(8,128)S(1)}, f32[32,128]{1,0:T(8,128)S(1)}, u32[]{:S(2)}, u32[]{:S(2)}) collective-permute-start(f32[32,128]{1,0:T(8,128)S(1)} %get-tuple-element.23.refs_0_), channel_id=1, source_target_pairs={{0,9},{1,8},{4,13},{5,12},{8,5},{9,4},{12,1},{13,0},{2,11},{3,10},... | collective-permute-start | bytes 49160 | tf_op jit(solution)/shard_map/ppermute | solution.py:369
  8.6 1.1 %collective-permute-start.3 = (f32[32,128]{1,0:T(8,128)S(1)}, f32[32,128]{1,0:T(8,128)S(1)}, u32[]{:S(2)}, u32[]{:S(2)}) collective-permute-start(f32[32,128]{1,0:T(8,128)S(1)} %get-tuple-element.23.refs_0_), channel_id=1, source_target_pairs={{0,13},{1,12},{4,9},{5,8},{8,1},{9,0},{12,5},{13,4},{2,15},{3,14},... | collective-permute-start | bytes 49160 | tf_op jit(solution)/shard_map/ppermute | solution.py:369
  9.7 0.4 %collective-permute-start.2 = (f32[32,128]{1,0:T(8,128)S(1)}, f32[32,128]{1,0:T(8,128)S(1)}, u32[]{:S(2)}, u32[]{:S(2)}) collective-permute-start(f32[32,128]{1,0:T(8,128)S(1)} %get-tuple-element.23.refs_0_), channel_id=1, source_target_pairs={{0,5},{1,4},{4,1},{5,0},{8,13},{9,12},{12,9},{13,8},{2,7},{3,6},{6... | collective-permute-start | bytes 49160 | tf_op jit(solution)/shard_map/ppermute | solution.py:369
  10.1 1.3 %first_columns.1 = (bf16[1024,1024]{1,0:T(8,128)(2,1)S(1)}, bf16[1024,768]{1,0:T(8,128)(2,1)S(1)}) custom-call(bf16[2048,512]{1,0:T(8,128)(2,1)S(1)} %get-tuple-element.18.refs_0_, bf16[2048,512]{1,0:T(8,128)(2,1)S(1)} %collective-permute-done.refs_1_, f32[64,128]{1,0:T(8,128)S(1)} %collective-permute-done.1.refs_2_, ...), custom_call_target="tpu_custom_call", output_to_operand_aliasing={{0}: (6, {}), {1}: (7, {})} | custom-call | flops 1610612736 | bytes 3670016 | tf_op jit(solution)/shard_map/first_columns/pallas_call | solution.py:457
  11.3 1.8 %second_columns.1 = (bf16[1024,768]{1,0:T(8,128)(2,1)S(1)}, bf16[1024,768]{1,0:T(8,128)(2,1)}) custom-call(bf16[1024,1024]{1,0:T(8,128)(2,1)S(1)} %get-tuple-element.28.masked_ref, s32[2,768]{1,0:T(2,128)S(1)} %get-tuple-element.21.refs_4_.slots_ref, s32[1]{0:T(128)S(6)} %copy.13.refs_5_.count_ref.refs_7_), custom_call_target="tpu_custom_call" | custom-call | flops 1610612736 | bytes 3670016 | tf_op jit(solution)/shard_map/second_columns/pallas_call | solution.py:468
  13.2 0.0 collective-permute-done.4.refs_3_
  13.2 0.0 collective-permute-done.3.refs_2_
  13.2 0.0 collective-permute-done.2.refs_1_
  13.2 1.5 %post_flows.1 = bf16[1024,768]{1,0:T(8,128)(2,1)} custom-call(f32[32,128]{1,0:T(8,128)S(1)} %get-tuple-element.23.refs_0_, f32[32,128]{1,0:T(8,128)S(1)} %collective-permute-done.2.refs_1_, f32[32,128]{1,0:T(8,128)S(1)} %collective-permute-done.3.refs_2_, f32[32,128]{1,0:T(8,128)S(1)} %collective-permute-done.4.refs_3_, ...), custom_call_target="tpu_custom_call", output_to_operand_aliasing={{}: (8, {})} | custom-call | flops 4718592 | bytes 1572864 | tf_op jit(solution)/shard_map/post_flows/pallas_call | solution.py:482
  (1 shorter events, 0.0 us)
Async XLA Ops:
  0.0 4.8 %collective-permute-start = (bf16[2048,512]{1,0:T(8,128)(2,1)}, bf16[2048,512]{1,0:T(8,128)(2,1)S(1)}, u32[]{:S(2)}, u32[]{:S(2)}) collective-permute-start(bf16[2048,512]{1,0:T(8,128)(2,1)} %d_hbm.1), channel_id=1, source_target_pairs={{0,1},{1,0},{2,3},{3,2},{4,5},{5,4},{6,7},{7,6},{8,9},{9,8},{10,11... | collective-permute-start | bytes 6291464 | tf_op jit(solution)/shard_map/ppermute | solution.py:401
  3.5 1.3 %collective-permute-start.1 = (f32[64,128]{1,0:T(8,128)S(1)}, f32[64,128]{1,0:T(8,128)S(1)}, u32[]{:S(2)}, u32[]{:S(2)}) collective-permute-start(f32[64,128]{1,0:T(8,128)S(1)} %get-tuple-element.19), channel_id=1, source_target_pairs={{0,1},{1,0},{2,3},{3,2},{4,5},{5,4},{6,7},{7,6},{8,9},{9,8},{10,11... | collective-permute-start | bytes 98312 | tf_op jit(solution)/shard_map/ppermute | solution.py:434
  5.6 7.6 %collective-permute-start.4 = (f32[32,128]{1,0:T(8,128)S(1)}, f32[32,128]{1,0:T(8,128)S(1)}, u32[]{:S(2)}, u32[]{:S(2)}) collective-permute-start(f32[32,128]{1,0:T(8,128)S(1)} %get-tuple-element.23.refs_0_), channel_id=1, source_target_pairs={{0,9},{1,8},{4,13},{5,12},{8,5},{9,4},{12,1},{13,0},{2,11},{3,10},... | collective-permute-start | bytes 49160 | tf_op jit(solution)/shard_map/ppermute | solution.py:369
  8.6 4.6 %collective-permute-start.3 = (f32[32,128]{1,0:T(8,128)S(1)}, f32[32,128]{1,0:T(8,128)S(1)}, u32[]{:S(2)}, u32[]{:S(2)}) collective-permute-start(f32[32,128]{1,0:T(8,128)S(1)} %get-tuple-element.23.refs_0_), channel_id=1, source_target_pairs={{0,13},{1,12},{4,9},{5,8},{8,1},{9,0},{12,5},{13,4},{2,15},{3,14},... | collective-permute-start | bytes 49160 | tf_op jit(solution)/shard_map/ppermute | solution.py:369
  9.7 3.5 %collective-permute-start.2 = (f32[32,128]{1,0:T(8,128)S(1)}, f32[32,128]{1,0:T(8,128)S(1)}, u32[]{:S(2)}, u32[]{:S(2)}) collective-permute-start(f32[32,128]{1,0:T(8,128)S(1)} %get-tuple-element.23.refs_0_), channel_id=1, source_target_pairs={{0,5},{1,4},{4,1},{5,0},{8,13},{9,12},{12,9},{13,8},{2,7},{3,6},{6... | collective-permute-start | bytes 49160 | tf_op jit(solution)/shard_map/ppermute | solution.py:369

commit v2 on v0

--- a/solution.py
+++ b/solution.py
@@ -125,14 +125,14 @@
             perm_ref[:, at * LANES : (at + 1) * LANES] = one_hot(
                 iota((ENDS, LANES), 0) + start == place[r : r + 1]
             )
+        for copy in copies:
+            copy.wait()
         packed = lax.dot_general(
             ends, perm_ref[...], (((1,), (1,)), ((), ())), preferred_element_type=F32
         ).astype(I32)
         end_col = packed[0:1] + (packed[1:2] << 8)
         end_row = packed[2:3] + (packed[3:4] << 8)
         hot_ref[...] = one_hot(iota((cols, ENDS), 0) == end_col)
-        for copy in copies:
-            copy.wait()
         keep = jnp.dot(
             mask_ref[...].astype(F32).astype(BF16), hot_ref[...], preferred_element_type=F32
         )
@@ -306,6 +306,8 @@
     shift_second = (flow_second + cross_second * flow_first) / determinant
     my_block = pl.multiple_of(lax.axis_index("sub") * my_blocks, my_blocks)
     base = jnp.swapaxes(base_ref[pl.ds(my_block, my_blocks), :], 0, 1)
+
+    per = 1 if my_blocks % 2 else 2
 
     def write(lines):
         live = [iota((1, LANES), 1) + line * LANES < count_ref[0] for line in lines]
@@ -330,12 +332,14 @@
                 post_ref[block, lanes] = jnp.where(
                     live[line], start + change.astype(F32), 0.0
                 ).astype(BF16)
-            out_copies.append(
-                pltpu.make_async_copy(
-                    post_ref.at[block, wide], out_hbm.at[block, wide], out_sems.at[b]
+            if (b + 1) % per == 0:
+                done = slice((b + 1 - per) * BLOCK, (b + 1) * BLOCK)
+                out_copies.append(
+                    pltpu.make_async_copy(
+                        post_ref.at[done, wide], out_hbm.at[done, wide], out_sems.at[b]
+                    )
                 )
-            )
-            out_copies[-1].start()
+                out_copies[-1].start()
         for copy in out_copies:
             copy.wait()
 

time: 14.6 us -> 15.1 us (1.034); the launches traced: 14.6 us -> 14.9 us
  Pallas kernels: 8.31 us -> 8.62 us
    pallas_call x1, Pallas kernels: 2.96 us -> 3.21 us  [on_device(): pl.pallas_call(functools.partial(values_kernel, n_sub), out_shape=[pltpu....]
where the time goes in v2:
time: 15.1 us; the launch traced here: 14.9 us
  Pallas kernels  8.62 us (57%)
  starting transfers between devices  5.06 us (34%)
  between operations  0.71 us (5%)
  waiting for transfers between devices  0.51 us (3%)
    ppermute x3, starting transfers between devices, from_other_mon(): lax.ppermute(share, ('mon', 'sub'), [(m * n_sub + s, to[m] * n_sub + n_su...  4.48 us
    pallas_call x1, Pallas kernels, on_device(): pl.pallas_call(functools.partial(values_kernel, n_sub), out_shape=[pltpu....  3.21 us
    pallas_call x1, Pallas kernels, on_device(): pl.pallas_call(functools.partial(second_kernel, n_sub), out_shape=[column...  1.85 us
    pallas_call x1, Pallas kernels, on_device(): pl.pallas_call(functools.partial(flows_kernel, len(shares), width), out_s...  1.55 us
    pallas_call x1, Pallas kernels, on_device(): pl.pallas_call(functools.partial(first_kernel, n_sub), out_shape=[pltpu.V...  1.26 us
    pallas_call x1, Pallas kernels, on_device(): pl.pallas_call(functools.partial(early_kernel, n_sub), out_shape=[masked,...  0.76 us
    ppermute x1, waiting for transfers between devices, on_device(): lax.ppermute(note, 'sub', ring)  0.5 us
    ppermute x1, starting transfers between devices, on_device(): lax.ppermute(dfactors, 'sub', ring)  0.45 us
  transfers between devices with their start and end apart: 5, of which 1 were waited for; matrix products, arithmetic and copies ran while one was open for 0% of the time, Pallas kernels for 42%

profile of v2, /device:TPU:0, one launch (start us, length us, event | category | flops | bytes accessed | tf_op | source)
XLA Modules:
  0.0 14.9 jit_solution(16357735939323982424)
XLA Ops:
  0.0 0.5 %collective-permute-start = (bf16[2048,512]{1,0:T(8,128)(2,1)}, bf16[2048,512]{1,0:T(8,128)(2,1)S(1)}, u32[]{:S(2)}, u32[]{:S(2)}) collective-permute-start(bf16[2048,512]{1,0:T(8,128)(2,1)} %d_hbm.1), channel_id=1, source_target_pairs={{0,1},{1,0},{2,3},{3,2},{4,5},{5,4},{6,7},{7,6},{8,9},{9,8},{10,11... | collective-permute-start | bytes 6291464 | tf_op jit(solution)/shard_map/ppermute | solution.py:399
  0.5 3.2 %pair_values.1 = (f32[32,128]{1,0:T(8,128)S(1)}, f32[64,128]{1,0:T(8,128)S(1)}, bf16[2048,512]{1,0:T(8,128)(2,1)S(1)}, s32[16,512]{1,0:T(8,128)S(1)}, f32[16,128]{1,0:T(8,128)S(1)}, /*index=5*/s32[2,768]{1,0:T(2,128)S(1)}) custom-call(bf16[2048,512]{1,0:T(8,128)(2,1)} %d_hbm.1, s32[16,512]{1,0:T(8,128)} %mask_hbm.1, f32[16,128]{1,0:T(8,128)} %bitcast.3, ...), custom_call_target="tpu_custom_call" | custom-call | flops 536870912 | bytes 2097152 | tf_op jit(solution)/shard_map/pair_values/pallas_call | solution.py:403
  3.7 0.1 collective-permute-start.1
  4.4 0.5 %collective-permute-done.1.refs_2_ = f32[64,128]{1,0:T(8,128)S(1)} collective-permute-done((f32[64,128]{1,0:T(8,128)S(1)}, f32[64,128]{1,0:T(8,128)S(1)}, u32[]{:S(2)}, u32[]{:S(2)}) %collective-permute-start.1) | collective-permute-done | bytes 32800 | tf_op jit(solution)/shard_map/ppermute | solution.py:432
  5.0 0.0 collective-permute-done.refs_1_
  5.0 0.8 %early_columns.1 = (bf16[1024,1024]{1,0:T(8,128)(2,1)S(1)}, bf16[1024,768]{1,0:T(8,128)(2,1)S(1)}, f32[32,128]{1,0:T(8,128)S(1)}) custom-call(bf16[2048,512]{1,0:T(8,128)(2,1)S(1)} %get-tuple-element.18.refs_0_, bf16[2048,512]{1,0:T(8,128)(2,1)S(1)} %collective-permute-done.refs_1_, f32[64,128]{1,0:T(8,128)S(1)} %collective-permute-done.1.refs_2_, ...), custom_call_target="tpu_custom_call" | custom-call | tf_op jit(solution)/shard_map/early_columns/pallas_call | solution.py:444
  5.7 3.0 %collective-permute-start.4 = (f32[32,128]{1,0:T(8,128)S(1)}, f32[32,128]{1,0:T(8,128)S(1)}, u32[]{:S(2)}, u32[]{:S(2)}) collective-permute-start(f32[32,128]{1,0:T(8,128)S(1)} %get-tuple-element.23.refs_0_), channel_id=1, source_target_pairs={{0,9},{1,8},{4,13},{5,12},{8,5},{9,4},{12,1},{13,0},{2,11},{3,10},... | collective-permute-start | bytes 49160 | tf_op jit(solution)/shard_map/ppermute | solution.py:367
  8.7 1.1 %collective-permute-start.3 = (f32[32,128]{1,0:T(8,128)S(1)}, f32[32,128]{1,0:T(8,128)S(1)}, u32[]{:S(2)}, u32[]{:S(2)}) collective-permute-start(f32[32,128]{1,0:T(8,128)S(1)} %get-tuple-element.23.refs_0_), channel_id=1, source_target_pairs={{0,13},{1,12},{4,9},{5,8},{8,1},{9,0},{12,5},{13,4},{2,15},{3,14},... | collective-permute-start | bytes 49160 | tf_op jit(solution)/shard_map/ppermute | solution.py:367
  9.8 0.4 %collective-permute-start.2 = (f32[32,128]{1,0:T(8,128)S(1)}, f32[32,128]{1,0:T(8,128)S(1)}, u32[]{:S(2)}, u32[]{:S(2)}) collective-permute-start(f32[32,128]{1,0:T(8,128)S(1)} %get-tuple-element.23.refs_0_), channel_id=1, source_target_pairs={{0,5},{1,4},{4,1},{5,0},{8,13},{9,12},{12,9},{13,8},{2,7},{3,6},{6... | collective-permute-start | bytes 49160 | tf_op jit(solution)/shard_map/ppermute | solution.py:367
  10.2 1.3 %first_columns.1 = (bf16[1024,1024]{1,0:T(8,128)(2,1)S(1)}, bf16[1024,768]{1,0:T(8,128)(2,1)S(1)}) custom-call(bf16[2048,512]{1,0:T(8,128)(2,1)S(1)} %get-tuple-element.18.refs_0_, bf16[2048,512]{1,0:T(8,128)(2,1)S(1)} %collective-permute-done.refs_1_, f32[64,128]{1,0:T(8,128)S(1)} %collective-permute-done.1.refs_2_, ...), custom_call_target="tpu_custom_call", output_to_operand_aliasing={{0}: (6, {}), {1}: (7, {})} | custom-call | flops 1610612736 | bytes 3670016 | tf_op jit(solution)/shard_map/first_columns/pallas_call | solution.py:455
  11.5 1.8 %second_columns.1 = (bf16[1024,768]{1,0:T(8,128)(2,1)S(1)}, bf16[1024,768]{1,0:T(8,128)(2,1)}) custom-call(bf16[1024,1024]{1,0:T(8,128)(2,1)S(1)} %get-tuple-element.28.masked_ref, s32[2,768]{1,0:T(2,128)S(1)} %get-tuple-element.21.refs_4_.slots_ref, s32[1]{0:T(128)S(6)} %copy.13.refs_5_.count_ref.refs_7_), custom_call_target="tpu_custom_call" | custom-call | flops 1610612736 | bytes 3670016 | tf_op jit(solution)/shard_map/second_columns/pallas_call | solution.py:466
  13.3 0.0 collective-permute-done.4.refs_3_
  13.3 0.0 collective-permute-done.3.refs_2_
  13.3 0.0 collective-permute-done.2.refs_1_
  13.4 1.5 %post_flows.1 = bf16[1024,768]{1,0:T(8,128)(2,1)} custom-call(f32[32,128]{1,0:T(8,128)S(1)} %get-tuple-element.23.refs_0_, f32[32,128]{1,0:T(8,128)S(1)} %collective-permute-done.2.refs_1_, f32[32,128]{1,0:T(8,128)S(1)} %collective-permute-done.3.refs_2_, f32[32,128]{1,0:T(8,128)S(1)} %collective-permute-done.4.refs_3_, ...), custom_call_target="tpu_custom_call", output_to_operand_aliasing={{}: (8, {})} | custom-call | flops 4718592 | bytes 1572864 | tf_op jit(solution)/shard_map/post_flows/pallas_call | solution.py:480
  (1 shorter events, 0.0 us)
Async XLA Ops:
  0.0 5.0 %collective-permute-start = (bf16[2048,512]{1,0:T(8,128)(2,1)}, bf16[2048,512]{1,0:T(8,128)(2,1)S(1)}, u32[]{:S(2)}, u32[]{:S(2)}) collective-permute-start(bf16[2048,512]{1,0:T(8,128)(2,1)} %d_hbm.1), channel_id=1, source_target_pairs={{0,1},{1,0},{2,3},{3,2},{4,5},{5,4},{6,7},{7,6},{8,9},{9,8},{10,11... | collective-permute-start | bytes 6291464 | tf_op jit(solution)/shard_map/ppermute | solution.py:399
  3.7 1.3 %collective-permute-start.1 = (f32[64,128]{1,0:T(8,128)S(1)}, f32[64,128]{1,0:T(8,128)S(1)}, u32[]{:S(2)}, u32[]{:S(2)}) collective-permute-start(f32[64,128]{1,0:T(8,128)S(1)} %get-tuple-element.19), channel_id=1, source_target_pairs={{0,1},{1,0},{2,3},{3,2},{4,5},{5,4},{6,7},{7,6},{8,9},{9,8},{10,11... | collective-permute-start | bytes 98312 | tf_op jit(solution)/shard_map/ppermute | solution.py:432
  5.7 7.6 %collective-permute-start.4 = (f32[32,128]{1,0:T(8,128)S(1)}, f32[32,128]{1,0:T(8,128)S(1)}, u32[]{:S(2)}, u32[]{:S(2)}) collective-permute-start(f32[32,128]{1,0:T(8,128)S(1)} %get-tuple-element.23.refs_0_), channel_id=1, source_target_pairs={{0,9},{1,8},{4,13},{5,12},{8,5},{9,4},{12,1},{13,0},{2,11},{3,10},... | collective-permute-start | bytes 49160 | tf_op jit(solution)/shard_map/ppermute | solution.py:367
  8.7 4.6 %collective-permute-start.3 = (f32[32,128]{1,0:T(8,128)S(1)}, f32[32,128]{1,0:T(8,128)S(1)}, u32[]{:S(2)}, u32[]{:S(2)}) collective-permute-start(f32[32,128]{1,0:T(8,128)S(1)} %get-tuple-element.23.refs_0_), channel_id=1, source_target_pairs={{0,13},{1,12},{4,9},{5,8},{8,1},{9,0},{12,5},{13,4},{2,15},{3,14},... | collective-permute-start | bytes 49160 | tf_op jit(solution)/shard_map/ppermute | solution.py:367
  9.8 3.5 %collective-permute-start.2 = (f32[32,128]{1,0:T(8,128)S(1)}, f32[32,128]{1,0:T(8,128)S(1)}, u32[]{:S(2)}, u32[]{:S(2)}) collective-permute-start(f32[32,128]{1,0:T(8,128)S(1)} %get-tuple-element.23.refs_0_), channel_id=1, source_target_pairs={{0,5},{1,4},{4,1},{5,0},{8,13},{9,12},{12,9},{13,8},{2,7},{3,6},{6... | collective-permute-start | bytes 49160 | tf_op jit(solution)/shard_map/ppermute | solution.py:367

commit v3 on v0

--- a/solution.py
+++ b/solution.py
@@ -81,7 +81,7 @@
         )
         for i in range(chunks)
     ]
-    for copy in small + large:
+    for copy in small[:2] + large + small[2:]:
         copy.start()
 
     small[0].wait()
@@ -197,6 +197,10 @@
     return min(2, parts)
 
 
+def zero_rows(rows):
+    return rows // BLOCK // 2 * BLOCK
+
+
 def live_parts(count, width, parts):
     return jnp.clip((count + width - 1) // width, fewest(parts), parts)
 
@@ -269,6 +273,7 @@
     slot = slots_ref[1:2, :]
     starts = column_starts(n_sub, cols)
     parts, _, width = hot_ref.shape
+    zero_start = masked_ref.shape[0] - zero_ref.shape[0]
     live = live_parts(count_ref[0], width, parts)
     for n_parts in range(fewest(parts), parts + 1):
 
@@ -276,7 +281,11 @@
         def _():
             copies = [
                 pltpu.make_async_copy(
-                    zero_ref, out_hbm.at[:, part * width : (part + 1) * width], sems.at[part]
+                    zero_ref,
+                    out_hbm.at[
+                        pl.ds(zero_start, zero_ref.shape[0]), part * width : (part + 1) * width
+                    ],
+                    sems.at[part],
                 )
                 for part in range(n_parts, parts)
             ]
@@ -316,10 +325,13 @@
             ]
             for shift in (shift_first, shift_second)
         ]
-        wide = slice(0, len(lines) * LANES)
         out_copies = []
         for b in range(my_blocks):
             block = slice(b * BLOCK, (b + 1) * BLOCK)
+            wide = slice(0, len(lines) * LANES)
+            if b * BLOCK < my_rows - zero_rows(my_rows) and wide.stop < cap:
+                post_ref[block, wide.stop :] = jnp.zeros((BLOCK, cap - wide.stop), BF16)
+                wide = slice(0, cap)
             start = jnp.broadcast_to(base[:, b : b + 1], (BLOCK, LANES))
             for line in lines:
                 lanes = slice(line * LANES, (line + 1) * LANES)
@@ -466,7 +478,7 @@
         out_specs=[vmem, hbm],
         scratch_shapes=[
             hot,
-            pltpu.VMEM((my_rows, width), BF16),
+            pltpu.VMEM((zero_rows(my_rows), width), BF16),
             pltpu.SemaphoreType.DMA((cap // width,)),
         ],
         compiler_params=params,

time: 14.6 us -> 14.6 us (level)
  no operation moved by 1% of the time
where the time goes in v3:
time: 14.6 us
  Pallas kernels  8.31 us (57%)
  starting transfers between devices  5.06 us (35%)
  between operations  0.71 us (5%)
  waiting for transfers between devices  0.51 us (3%)
    ppermute x3, starting transfers between devices, from_other_mon(): lax.ppermute(share, ('mon', 'sub'), [(m * n_sub + s, to[m] * n_sub + n_su...  4.48 us
    pallas_call x1, Pallas kernels, on_device(): pl.pallas_call(functools.partial(values_kernel, n_sub), out_shape=[pltpu....  2.96 us
    pallas_call x1, Pallas kernels, on_device(): pl.pallas_call(functools.partial(second_kernel, n_sub), out_shape=[column...  1.85 us
    pallas_call x1, Pallas kernels, on_device(): pl.pallas_call(functools.partial(flows_kernel, len(shares), width), out_s...  1.5 us
    pallas_call x1, Pallas kernels, on_device(): pl.pallas_call(functools.partial(first_kernel, n_sub), out_shape=[pltpu.V...  1.25 us
    pallas_call x1, Pallas kernels, on_device(): pl.pallas_call(functools.partial(early_kernel, n_sub), out_shape=[masked,...  0.75 us
    ppermute x1, waiting for transfers between devices, on_device(): lax.ppermute(note, 'sub', ring)  0.5 us
    ppermute x1, starting transfers between devices, on_device(): lax.ppermute(dfactors, 'sub', ring)  0.45 us
  transfers between devices with their start and end apart: 5, of which 1 were waited for; matrix products, arithmetic and copies ran while one was open for 0% of the time, Pallas kernels for 42%

profile of v3, /device:TPU:0, one launch (start us, length us, event | category | flops | bytes accessed | tf_op | source)
XLA Modules:
  0.0 14.6 jit_solution(9091650363619320005)
XLA Ops:
  0.0 0.5 %collective-permute-start = (bf16[2048,512]{1,0:T(8,128)(2,1)}, bf16[2048,512]{1,0:T(8,128)(2,1)S(1)}, u32[]{:S(2)}, u32[]{:S(2)}) collective-permute-start(bf16[2048,512]{1,0:T(8,128)(2,1)} %d_hbm.1), channel_id=1, source_target_pairs={{0,1},{1,0},{2,3},{3,2},{4,5},{5,4},{6,7},{7,6},{8,9},{9,8},{10,11... | collective-permute-start | bytes 6291464 | tf_op jit(solution)/shard_map/ppermute | solution.py:407
  0.5 3.0 %pair_values.1 = (f32[32,128]{1,0:T(8,128)S(1)}, f32[64,128]{1,0:T(8,128)S(1)}, bf16[2048,512]{1,0:T(8,128)(2,1)S(1)}, s32[16,512]{1,0:T(8,128)S(1)}, f32[16,128]{1,0:T(8,128)S(1)}, /*index=5*/s32[2,768]{1,0:T(2,128)S(1)}) custom-call(bf16[2048,512]{1,0:T(8,128)(2,1)} %d_hbm.1, s32[16,512]{1,0:T(8,128)} %mask_hbm.1, f32[16,128]{1,0:T(8,128)} %bitcast.3, ...), custom_call_target="tpu_custom_call" | custom-call | flops 536870912 | bytes 2097152 | tf_op jit(solution)/shard_map/pair_values/pallas_call | solution.py:411
  3.4 0.1 collective-permute-start.1
  4.2 0.5 %collective-permute-done.1.refs_2_ = f32[64,128]{1,0:T(8,128)S(1)} collective-permute-done((f32[64,128]{1,0:T(8,128)S(1)}, f32[64,128]{1,0:T(8,128)S(1)}, u32[]{:S(2)}, u32[]{:S(2)}) %collective-permute-start.1) | collective-permute-done | bytes 32800 | tf_op jit(solution)/shard_map/ppermute | solution.py:440
  4.7 0.0 collective-permute-done.refs_1_
  4.7 0.8 %early_columns.1 = (bf16[1024,1024]{1,0:T(8,128)(2,1)S(1)}, bf16[1024,768]{1,0:T(8,128)(2,1)S(1)}, f32[32,128]{1,0:T(8,128)S(1)}) custom-call(bf16[2048,512]{1,0:T(8,128)(2,1)S(1)} %get-tuple-element.18.refs_0_, bf16[2048,512]{1,0:T(8,128)(2,1)S(1)} %collective-permute-done.refs_1_, f32[64,128]{1,0:T(8,128)S(1)} %collective-permute-done.1.refs_2_, ...), custom_call_target="tpu_custom_call" | custom-call | tf_op jit(solution)/shard_map/early_columns/pallas_call | solution.py:452
  5.5 3.0 %collective-permute-start.4 = (f32[32,128]{1,0:T(8,128)S(1)}, f32[32,128]{1,0:T(8,128)S(1)}, u32[]{:S(2)}, u32[]{:S(2)}) collective-permute-start(f32[32,128]{1,0:T(8,128)S(1)} %get-tuple-element.23.refs_0_), channel_id=1, source_target_pairs={{0,9},{1,8},{4,13},{5,12},{8,5},{9,4},{12,1},{13,0},{2,11},{3,10},... | collective-permute-start | bytes 49160 | tf_op jit(solution)/shard_map/ppermute | solution.py:375
  8.5 1.1 %collective-permute-start.3 = (f32[32,128]{1,0:T(8,128)S(1)}, f32[32,128]{1,0:T(8,128)S(1)}, u32[]{:S(2)}, u32[]{:S(2)}) collective-permute-start(f32[32,128]{1,0:T(8,128)S(1)} %get-tuple-element.23.refs_0_), channel_id=1, source_target_pairs={{0,13},{1,12},{4,9},{5,8},{8,1},{9,0},{12,5},{13,4},{2,15},{3,14},... | collective-permute-start | bytes 49160 | tf_op jit(solution)/shard_map/ppermute | solution.py:375
  9.6 0.4 %collective-permute-start.2 = (f32[32,128]{1,0:T(8,128)S(1)}, f32[32,128]{1,0:T(8,128)S(1)}, u32[]{:S(2)}, u32[]{:S(2)}) collective-permute-start(f32[32,128]{1,0:T(8,128)S(1)} %get-tuple-element.23.refs_0_), channel_id=1, source_target_pairs={{0,5},{1,4},{4,1},{5,0},{8,13},{9,12},{12,9},{13,8},{2,7},{3,6},{6... | collective-permute-start | bytes 49160 | tf_op jit(solution)/shard_map/ppermute | solution.py:375
  9.9 1.3 %first_columns.1 = (bf16[1024,1024]{1,0:T(8,128)(2,1)S(1)}, bf16[1024,768]{1,0:T(8,128)(2,1)S(1)}) custom-call(bf16[2048,512]{1,0:T(8,128)(2,1)S(1)} %get-tuple-element.18.refs_0_, bf16[2048,512]{1,0:T(8,128)(2,1)S(1)} %collective-permute-done.refs_1_, f32[64,128]{1,0:T(8,128)S(1)} %collective-permute-done.1.refs_2_, ...), custom_call_target="tpu_custom_call", output_to_operand_aliasing={{0}: (6, {}), {1}: (7, {})} | custom-call | flops 1610612736 | bytes 3670016 | tf_op jit(solution)/shard_map/first_columns/pallas_call | solution.py:463
  11.2 1.8 %second_columns.1 = (bf16[1024,768]{1,0:T(8,128)(2,1)S(1)}, bf16[1024,768]{1,0:T(8,128)(2,1)}) custom-call(bf16[1024,1024]{1,0:T(8,128)(2,1)S(1)} %get-tuple-element.28.masked_ref, s32[2,768]{1,0:T(2,128)S(1)} %get-tuple-element.21.refs_4_.slots_ref, s32[1]{0:T(128)S(6)} %copy.13.refs_5_.count_ref.refs_7_), custom_call_target="tpu_custom_call" | custom-call | flops 1610612736 | bytes 3670016 | tf_op jit(solution)/shard_map/second_columns/pallas_call | solution.py:474
  13.1 0.0 collective-permute-done.4.refs_3_
  13.1 0.0 collective-permute-done.3.refs_2_
  13.1 0.0 collective-permute-done.2.refs_1_
  13.1 1.5 %post_flows.1 = bf16[1024,768]{1,0:T(8,128)(2,1)} custom-call(f32[32,128]{1,0:T(8,128)S(1)} %get-tuple-element.23.refs_0_, f32[32,128]{1,0:T(8,128)S(1)} %collective-permute-done.2.refs_1_, f32[32,128]{1,0:T(8,128)S(1)} %collective-permute-done.3.refs_2_, f32[32,128]{1,0:T(8,128)S(1)} %collective-permute-done.4.refs_3_, ...), custom_call_target="tpu_custom_call", output_to_operand_aliasing={{}: (8, {})} | custom-call | flops 4718592 | bytes 1572864 | tf_op jit(solution)/shard_map/post_flows/pallas_call | solution.py:488
  (1 shorter events, 0.0 us)
Async XLA Ops:
  0.0 4.7 %collective-permute-start = (bf16[2048,512]{1,0:T(8,128)(2,1)}, bf16[2048,512]{1,0:T(8,128)(2,1)S(1)}, u32[]{:S(2)}, u32[]{:S(2)}) collective-permute-start(bf16[2048,512]{1,0:T(8,128)(2,1)} %d_hbm.1), channel_id=1, source_target_pairs={{0,1},{1,0},{2,3},{3,2},{4,5},{5,4},{6,7},{7,6},{8,9},{9,8},{10,11... | collective-permute-start | bytes 6291464 | tf_op jit(solution)/shard_map/ppermute | solution.py:407
  3.4 1.3 %collective-permute-start.1 = (f32[64,128]{1,0:T(8,128)S(1)}, f32[64,128]{1,0:T(8,128)S(1)}, u32[]{:S(2)}, u32[]{:S(2)}) collective-permute-start(f32[64,128]{1,0:T(8,128)S(1)} %get-tuple-element.19), channel_id=1, source_target_pairs={{0,1},{1,0},{2,3},{3,2},{4,5},{5,4},{6,7},{7,6},{8,9},{9,8},{10,11... | collective-permute-start | bytes 98312 | tf_op jit(solution)/shard_map/ppermute | solution.py:440
  5.5 7.6 %collective-permute-start.4 = (f32[32,128]{1,0:T(8,128)S(1)}, f32[32,128]{1,0:T(8,128)S(1)}, u32[]{:S(2)}, u32[]{:S(2)}) collective-permute-start(f32[32,128]{1,0:T(8,128)S(1)} %get-tuple-element.23.refs_0_), channel_id=1, source_target_pairs={{0,9},{1,8},{4,13},{5,12},{8,5},{9,4},{12,1},{13,0},{2,11},{3,10},... | collective-permute-start | bytes 49160 | tf_op jit(solution)/shard_map/ppermute | solution.py:375
  8.5 4.6 %collective-permute-start.3 = (f32[32,128]{1,0:T(8,128)S(1)}, f32[32,128]{1,0:T(8,128)S(1)}, u32[]{:S(2)}, u32[]{:S(2)}) collective-permute-start(f32[32,128]{1,0:T(8,128)S(1)} %get-tuple-element.23.refs_0_), channel_id=1, source_target_pairs={{0,13},{1,12},{4,9},{5,8},{8,1},{9,0},{12,5},{13,4},{2,15},{3,14},... | collective-permute-start | bytes 49160 | tf_op jit(solution)/shard_map/ppermute | solution.py:375
  9.6 3.5 %collective-permute-start.2 = (f32[32,128]{1,0:T(8,128)S(1)}, f32[32,128]{1,0:T(8,128)S(1)}, u32[]{:S(2)}, u32[]{:S(2)}) collective-permute-start(f32[32,128]{1,0:T(8,128)S(1)} %get-tuple-element.23.refs_0_), channel_id=1, source_target_pairs={{0,5},{1,4},{4,1},{5,0},{8,13},{9,12},{12,9},{13,8},{2,7},{3,6},{6... | collective-permute-start | bytes 49160 | tf_op jit(solution)/shard_map/ppermute | solution.py:375
